TPU v7x, 256 devices: a whole 4x4x8 slice. The times are simulated.
256 devices in a mesh: tm: 8 (over z), orb: 4 (over y_hi, core), aux: 8 (over y_lo, x).
Axes of the slice: x: 4, y: 4 (y_hi: 2, y_lo: 2; y = y_hi * 2 + y_lo), z: 8, core: 2. Of those that a mesh axis runs over, the one named last changes fastest.
Arguments:
- three_center: bfloat16 [1024, 6, 4096], P('orb', None, 'aux'), may hold values from -1.5 to 1.5
- block_mask: int32 [16, 6, 32], P('orb', None, 'aux'), may hold values from 0 to 1, as said below
- green_functions: bfloat16 [8, 1024, 1024], P('tm', 'orb'), may hold values from -0.1875 to 0.1875
- time_slot: int32 [4], replicated, may hold values from 0 to 3, each once
- grid_times: float32 [4], replicated, may hold values from 0.3 to 3
- grid_frequencies: float32 [4], replicated, may hold values from 0.3 to 3
- cosine_weights: float32 [4, 4], replicated, may hold values from 0.5 to 1.5
Outputs:
- chi_freq: float32 [4096, 4, 4096], P(('tm', 'orb'), None, 'aux')
Inputs may be any that keep to these rules, and one draw needn't show every extreme that they name: `block_mask`: 0 or 1. The share of present blocks may differ from one slice of 512 auxiliary functions to another. `time_slot`: each grid time point stands once.
All inputs are finite; a program needn't handle non-finite values.
Results may differ from a plain program's by a relative error of at most 0.004.
Values may be sent and summed in bfloat16 or wider, within the bound.
A program may use at most 64 MiB of HBM per device.

v0:
```python
import jax
import jax.numpy as jnp
from jax import lax
from jax.sharding import PartitionSpec as P


def from_partner(value, axis, stride):
    return lax.ppermute(value, axis, [(i, i ^ 1 << stride) for i in range(lax.axis_size(axis))])


def pair_term(other_side, shard_piece):
    return lax.dot_general(
        shard_piece, other_side, (((0, 1), (0, 1)), ((), ())), preferred_element_type=jnp.float32
    )


def per_device(
    three_center,
    block_mask,
    green_functions,
    time_slot,
    grid_times,
    grid_frequencies,
    cosine_weights,
):
    local_rows, nbatch, aux_local = three_center.shape
    mask_rows = block_mask.shape[0]
    aux_blocks = block_mask.shape[2]
    orb_count = lax.axis_size("orb")
    tm_count = lax.axis_size("tm")
    expanded = three_center.reshape(
        mask_rows, local_rows // mask_rows, nbatch, aux_blocks, aux_local // aux_blocks
    )
    expanded = expanded * block_mask.astype(jnp.bfloat16)[:, None, :, :, None]
    expanded = expanded.reshape(local_rows, nbatch, aux_local)
    flat_rows = expanded.reshape(local_rows, nbatch * aux_local)
    own_green = green_functions[0]
    contract = (((0,), (0,)), ((), ()))
    summed = lax.psum_scatter(
        lax.dot_general(own_green, flat_rows, contract, preferred_element_type=jnp.float32),
        "orb",
        scatter_dimension=0,
        tiled=True,
    )
    half_done = summed.astype(jnp.bfloat16).reshape(local_rows, nbatch, aux_local)
    partner = from_partner(half_done, "tm", 0)
    partial_chi = pair_term(half_done, lax.all_gather(partner, "aux", axis=2, tiled=True))
    time_count = time_slot.shape[0]
    cosine_table = cosine_weights * jnp.cos(grid_frequencies[:, None] * grid_times[None, :])
    slot_match = (time_slot[:, None] == jnp.arange(time_count, dtype=jnp.int32)[None, :]).astype(
        jnp.float32
    )
    pair_coefs = jnp.dot(cosine_table, slot_match.T, precision=lax.Precision.HIGHEST)
    weights = 0.5 * jnp.repeat(pair_coefs, 2, axis=1)
    out_rows = partial_chi.shape[0] // (tm_count * orb_count)
    blocks = lax.all_to_all(partial_chi, ("tm", "orb"), split_axis=0, concat_axis=0, tiled=True)
    blocks = jnp.sum(blocks.reshape(tm_count, orb_count, out_rows, aux_local), axis=1)
    result = jnp.einsum("jt,tqp->qjp", weights, blocks, precision=lax.Precision.HIGHEST)
    return result


def solution(mesh):
    return jax.shard_map(
        per_device,
        mesh=mesh,
        in_specs=(
            P("orb", None, "aux"),
            P("orb", None, "aux"),
            P("tm", "orb", None),
            P(),
            P(),
            P(),
            P(),
        ),
        out_specs=P(("tm", "orb"), None, "aux"),
        check_vma=False,
    )
```

profile of v0, /device:TPU:1, one launch (start us, length us, event | category | flops | bytes accessed | tf_op | source)
XLA Modules:
  0.0 535.0 jit_solution(17758503294725766863)
XLA Ops:
  6.5 0.0 copy-start
  6.5 0.0 reduce-scatter.2.cloned.1.call-start
  6.5 0.8 convert_element_type.7
  7.3 0.1 copy.23
  7.4 0.5 mul.40
  7.9 2.0 mul.41
  10.0 3.5 mul.42
  13.5 1.7 copy.24
  15.2 0.0 copy-done
  15.2 6.3 %convolution_bitcast_fusion = f32[1024,3072]{0,1:T(8,128)} fusion(bf16[256,3072]{0,1:T(8,128)(2,1)S(1)} %bitcast.29, bf16[1,256,1024]{2,1,0:T(8,128)(2,1)S(1)} %copy-done), kind=kOutput, calls=%fused_computation.1 | convolution fusion | flops 1610612736 | bytes 14680064 | tf_op jit(solution)/shard_map/dot_general | solution.py:40
  21.5 0.0 reduce-scatter.2.cloned.1.call-update
  21.6 0.0 all-gather.2.cloned.1.call-start
  21.6 115.0 %reduce-scatter.2.cloned.1.call-done = f32[256,3072]{0,1:T(8,128)} async-done(((f32[1024,3072]{0,1:T(8,128)}), f32[256,3072]{0,1:T(8,128)}) %reduce-scatter.2.cloned.1.call-update) | async-done | bytes 3145744 | tf_op jit(solution)/shard_map/reduce_scatter | solution.py:39
  136.6 2.0 convert_element_type.8
  138.7 0.0 copy-start.2
  138.7 1.2 copy-done.2
  139.9 1.3 collective-permute-start
  141.1 33.9 %collective-permute-done = bf16[256,6,512]{0,2,1:T(8,128)(2,1)S(1)} collective-permute-done((bf16[256,6,512]{0,2,1:T(8,128)(2,1)S(1)}, bf16[256,6,512]{0,2,1:T(8,128)(2,1)S(1)}, u32[]{:S(2)}, u32[]{:S(2)}) %collective-permute-start) | collective-permute-done | bytes 1572896 | tf_op jit(solution)/shard_map/ppermute | solution.py:8
  175.1 1.2 copy-done.1
  176.3 0.0 all-gather.2.cloned.1.call-update
  176.3 134.2 %all-gather.2.cloned.1.call-done = bf16[256,6,4096]{0,2,1:T(8,128)(2,1)} async-done(((bf16[256,6,512]{0,2,1:T(8,128)(2,1)}), bf16[256,6,4096]{0,2,1:T(8,128)(2,1)}) %all-gather.2.cloned.1.call-update) | async-done | bytes 12582928 | tf_op jit(solution)/shard_map/all_gather | solution.py:47
  310.5 12.2 %convolution_bitcast_fusion.1 = f32[32,128,512]{2,1,0:T(8,128)} fusion(bf16[32,128,256,6]{2,1,0,3:T(8,128)(2,1)} %bitcast.33, bf16[256,6,512,1]{0,2,3,1:T(8,128)(2,1)} %bitcast.31), kind=kOutput, calls=%fused_computation.2 | convolution fusion | flops 6442450944 | bytes 22544384 | tf_op jit(solution)/shard_map/dot_general | solution.py:12
  322.7 0.0 copy-start.6
  322.7 10.2 %all-to-all-start = ((f32[32,128,512]{2,1,0:T(8,128)}), f32[32,128,512]{2,1,0:T(8,128)}, u32[]{:S(2)}, u32[]{:S(2)}) async-start(f32[32,128,512]{2,1,0:T(8,128)} %convolution_bitcast_fusion.1), calls=%async_computation.1 | async-start | bytes 16777216 | tf_op jit(solution)/shard_map/all_to_all | solution.py:56
  332.9 0.0 copy-done.3
  332.9 0.0 copy-done.4
  332.9 0.0 copy-done.5
  332.9 0.2 convolution_multiply_fusion
  333.2 0.1 copy.26
  333.3 186.2 %all-to-all-done = f32[32,128,512]{2,1,0:T(8,128)} async-done(((f32[32,128,512]{2,1,0:T(8,128)}), f32[32,128,512]{2,1,0:T(8,128)}, u32[]{:S(2)}, u32[]{:S(2)}) %all-to-all-start) | async-done | bytes 8388640 | tf_op jit(solution)/shard_map/all_to_all | solution.py:56
  519.5 4.6 bitcast_reduce_fusion
  524.1 4.0 fusion.2
  (6 shorter events, 0.0 us)
Async XLA Ops:
  6.5 8.7 %copy-start = (bf16[1,256,1024]{2,1,0:T(8,128)(2,1)S(1)}, bf16[1,256,1024]{2,1,0:T(8,128)(2,1)}, u32[]{:S(2)}) copy-start(bf16[1,256,1024]{2,1,0:T(8,128)(2,1)} %param.9) | copy-start | bytes 1572868
  6.5 130.1 %reduce-scatter.2.cloned.1.call-start = ((), (), s32[]{:S(2)}) async-start(), calls=%async_computation.2 | async-start | bytes 15728640 | tf_op jit(solution)/shard_map/reduce_scatter | solution.py:39
  21.6 288.9 %all-gather.2.cloned.1.call-start = ((), (), s32[]{:S(2)}) async-start(), calls=%async_computation.3 | async-start | bytes 14155776 | tf_op jit(solution)/shard_map/all_gather | solution.py:47
  138.7 1.2 copy-start.2
  139.9 35.2 %collective-permute-start = (bf16[256,6,512]{0,2,1:T(8,128)(2,1)S(1)}, bf16[256,6,512]{0,2,1:T(8,128)(2,1)S(1)}, u32[]{:S(2)}, u32[]{:S(2)}) collective-permute-start(bf16[256,6,512]{0,2,1:T(8,128)(2,1)S(1)} %bitcast.30), channel_id=1, source_target_pairs={{0,32},{32,0},{64,96},{96,64},{128,160},{160,128},{192,224},{224,1... | collective-permute-start | bytes 4718600 | tf_op jit(solution)/shard_map/ppermute | solution.py:8
  175.1 1.2 copy-start.1
  322.7 10.2 %copy-start.3 = (f32[4,4]{1,0:T(4,128)S(1)}, f32[4,4]{1,0:T(4,128)}, u32[]{:S(2)}) copy-start(f32[4,4]{1,0:T(4,128)} %param.13) | copy-start | bytes 196
  322.7 10.2 %copy-start.4 = (s32[4]{0:T(128)S(1)}, s32[4]{0:T(128)}, u32[]{:S(2)}) copy-start(s32[4]{0:T(128)} %param.10) | copy-start | bytes 52
  322.7 10.3 %copy-start.5 = (f32[4]{0:T(128)S(1)}, f32[4]{0:T(128)}, u32[]{:S(2)}) copy-start(f32[4]{0:T(128)} %param.11) | copy-start | bytes 52
  322.7 10.3 %copy-start.6 = (f32[4]{0:T(128)S(1)}, f32[4]{0:T(128)}, u32[]{:S(2)}) copy-start(f32[4]{0:T(128)} %param.12) | copy-start | bytes 52
  322.7 196.8 %all-to-all-start = ((f32[32,128,512]{2,1,0:T(8,128)}), f32[32,128,512]{2,1,0:T(8,128)}, u32[]{:S(2)}, u32[]{:S(2)}) async-start(f32[32,128,512]{2,1,0:T(8,128)} %convolution_bitcast_fusion.1), calls=%async_computation.1 | async-start | bytes 16777216 | tf_op jit(solution)/shard_map/all_to_all | solution.py:56
Sparse Core Ops, SparseCore 0:
  21.7 114.9 reduce-scatter.1
  176.4 134.0 all-gather.1
where the time goes:
time: 535 us
  waiting for transfers between devices  469 us (88%)
  matrix products  22.7 us (4%)
  between operations  13.5 us (3%)
  starting transfers between devices  11.5 us (2%)
  other arithmetic  11 us (2%)
  local copies, waits for them, and re-layouts  6.8 us (1%)
    all_to_all x1, waiting for transfers between devices, per_device(): lax.all_to_all(partial_chi, ('tm', 'orb'), split_axis=0, concat_axis=0, t...  186 us
    all_gather x1, waiting for transfers between devices, per_device(): lax.all_gather(partner, 'aux', axis=2, tiled=True)  134 us
    reduce_scatter x1, waiting for transfers between devices, per_device(): lax.psum_scatter(lax.dot_general(own_green, flat_rows, contract, preferre...  115 us
    ppermute x1, waiting for transfers between devices, from_partner(): lax.ppermute(value, axis, [(i, i ^ 1 << stride) for i in range(lax.axis_s...  33.9 us
    dot_general x1, matrix products, pair_term(): lax.dot_general(shard_piece, other_side, (((0, 1), (0, 1)), ((), ())), pr...  12.2 us
  transfers between devices with their start and end apart: 4, of which 4 were waited for; matrix products, arithmetic and copies ran while one was open for 0% of the time, Pallas kernels for 0%

commit v1 on v0

v1 whole, which is shorter than its diff:
```python
import jax
import jax.numpy as jnp
from jax import lax
from jax.experimental import pallas as pl
from jax.experimental.pallas import tpu as pltpu
from jax.sharding import PartitionSpec as P

MESH = pl.DeviceIdType.MESH
F32 = jnp.float32
BF16 = jnp.bfloat16

CHILD = (3985, 272, 224, 2192)
DEPTH = (23130, 7146, 58372)
DEEPEST = 5
STEPS = ((1, 0), (0, 1), (-1, 0), (0, -1))


def bit_of(table, place):
    return lax.shift_right_logical(jnp.int32(table), place) & 1


def hops_up(j):
    return 4 if j < 2 else 3


def hops_down(j):
    return 3 if j < 2 else 4


def kernel(
    m_ref, mask_ref, g_ref, w_ref, out_ref,
    mp, mq, mqt, tbuf, gc, es, er, tmy, nt, acc, sbuf, rbuf,
    sib_s, sib_r, g_s, g_r, own_sem, tree_s, tree_r, e_s, e_r, pl_s, pl_r, z_s, z_r, ts_s, ts_r, o_s, o_r,
):
    nb = m_ref.shape[0]
    chunks = 2 * nb
    z = lax.axis_index("tm")
    orb = lax.axis_index("orb")
    aux = lax.axis_index("aux")
    yh, c = orb // 2, orb % 2
    yl, x = aux // 4, aux % 4
    y = 2 * yh + yl

    def dev(dx, dy, dz, core):
        ny = (y + dy) % 4
        return ((z + dz) % 8, (ny // 2) * 2 + core, (ny % 2) * 4 + (x + dx) % 4)

    def remote(src, dst, s, r, where):
        return pltpu.make_async_remote_copy(
            src_ref=src, dst_ref=dst, send_sem=s, recv_sem=r, device_id=where, device_id_type=MESH
        )

    sibling = (z, yh * 2 + 1 - c, aux)
    partner = (z, (1 - yh) * 2 + c, aux)
    zpair = z + 1 - 2 * (z % 2)
    swapped = [(zpair, yl * 2 + core, yh * 4 + x) for core in range(2)]

    barrier = pltpu.get_barrier_semaphore()
    greet = [sibling, partner] + swapped
    greet += [((z + d) % 8, orb, aux) for d in range(1, 8)]
    greet += [(z, orb, (aux + d) % 8) for d in range(1, 8)]
    other_y = (y + 3 + 2 * (y % 2)) % 4
    greet += [(z, (other_y // 2) * 2 + c, (other_y % 2) * 4 + x)]
    for where in greet:
        pl.semaphore_signal(barrier, inc=1, device_id=where, device_id_type=MESH)
    pl.semaphore_wait(barrier, len(greet))

    half_rows = pl.ds(pl.multiple_of((x % 2) * 128, 128), 128)
    g_copies = [remote(g_ref.at[half_rows, :], gc, g_s.at[core], g_r, swapped[core]) for core in range(2)]

    @pl.when(c == x // 2)
    def _():
        for copy in g_copies:
            copy.start()

    def sib_copy(n):
        mine = pl.ds(pl.multiple_of(c * 256, 256), 256)
        return remote(mp.at[n, mine, :], mp.at[n, mine, :], sib_s.at[n], sib_r.at[n], sibling)

    for n in range(nb):
        for b in range(4):
            for ab in range(4):
                present = jnp.full((64, 128), mask_ref[b, n, ab].astype(F32), F32).astype(BF16)
                rows = pl.ds(pl.multiple_of(c * 256 + b * 64, 64), 64)
                mp[n, rows, ab * 128:(ab + 1) * 128] = (
                    m_ref[n, b * 64:(b + 1) * 64, ab * 128:(ab + 1) * 128] * present
                )
        sib_copy(n).start()

    rx = (x + 4 - z % 4) % 4
    depth, child, is_root = [], [], []
    for s in range(2):
        ry = (y + 8 - z // 4 - 2 * s) % 4
        px, py = rx, ry
        for t in range(4):
            place = px * 4 + py
            depth.append(bit_of(DEPTH[0], place) + 2 * bit_of(DEPTH[1], place) + 4 * bit_of(DEPTH[2], place))
            child.append([bit_of(CHILD[(e - t) % 4], place) for e in range(4)])
            px, py = py, (4 - px) % 4
        is_root.append((rx + ry) == 0)
    neighbours = [dev(dx, dy, 0, c) for dx, dy in STEPS]

    def tree_copy(s, t, q, e, root):
        n, qb = q // 2, q % 2
        dst = mq.at[n, qb, pl.ds(s * 512 + t * 128, 128), :]
        if root:
            src = mp.at[n, pl.ds(t * 128, 128), pl.ds(pl.multiple_of((c + 2 * qb) * 128, 128), 128)]
        else:
            src = dst
        return remote(src, dst, tree_s.at[4 * s + t, e, q], tree_r.at[4 * s + t, q], neighbours[e])

    def tree_step(k):
        @pl.when(k < nb)
        def _():
            sib_copy(k).wait_recv()

        for s in range(2):
            @pl.when(is_root[s] & (k < chunks))
            def _(s=s):
                for t in range(4):
                    tree_copy(s, t, k, t, True).start()

            for t in range(4):
                q = k - depth[4 * s + t]

                @pl.when((depth[4 * s + t] > 0) & (q >= 0) & (q < chunks))
                def _(s=s, t=t, q=q):
                    tree_copy(s, t, q, 0, False).wait_recv()
                    for e in range(4):
                        @pl.when(child[4 * s + t][e] == 1)
                        def _(e=e):
                            tree_copy(s, t, q, e, False).start()

    def tree_sends_done(q):
        for s in range(2):
            for t in range(4):
                for e in range(4):
                    @pl.when(child[4 * s + t][e] == 1)
                    def _(s=s, t=t, e=e):
                        tree_copy(s, t, q, e, False).wait_send()

    def e_copy(d):
        to = (z + d) % 8
        return remote(
            es.at[pl.ds(pl.multiple_of(to * 16, 16), 16), :], er.at[z], e_s.at[d - 1], e_r.at[d - 1], (to, orb, aux)
        )

    def plane_copy(d):
        return remote(
            tmy, tbuf.at[:, c, aux, z], pl_s.at[d - 1], pl_r.at[d - 1], (z, orb, (aux + d) % 8)
        )

    def z_copy(j, h, up):
        origin = (z + 8 - h) % 8 if up else (z + h) % 8
        to = (z + 1) % 8 if up else (z + 7) % 8
        way = 0 if up else 1
        piece = tbuf.at[j, c, :, origin]
        return remote(piece, piece, z_s.at[way, j, h], z_r.at[way, j, h], (to, orb, aux))

    def z_event(j, h):
        for up in (True, False):
            if h < (hops_up(j) if up else hops_down(j)):
                if h > 0:
                    z_copy(j, h - 1, up).wait_recv()
                z_copy(j, h, up).start()

    def t_done(j):
        z_copy(j, hops_up(j) - 1, True).wait_recv()
        z_copy(j, hops_down(j) - 1, False).wait_recv()
        remote(tbuf.at[j, c], tbuf.at[j, c], ts_s.at[j], ts_r.at[j], sibling).start()

    def phase_e():
        remote(g_ref.at[half_rows, :], gc, g_s.at[0], g_r, swapped[0]).wait_recv()
        es[...] = lax.dot_general(gc[...], g_ref[...], (((1,), (1,)), ((), ())), preferred_element_type=F32)
        for d in range(1, 8):
            e_copy(d).start()
        er[z] = es[pl.ds(pl.multiple_of(z * 16, 16), 16), :]

    def phase_t():
        for d in range(1, 8):
            e_copy(d).wait_recv()
        for j in range(4):
            total = w_ref[j, 0] * er[0]
            for s in range(1, 8):
                total = total + w_ref[j, s] * er[s]
            tmy[j] = total.astype(BF16)
        for d in range(1, 8):
            plane_copy(d).start()
        tbuf[:, c, aux, z] = tmy[...]

    def phase_plane():
        for d in range(1, 8):
            plane_copy(d).wait_recv()

    def own_copy(n, qb):
        return pltpu.make_async_copy(
            mp.at[n, :, pl.ds(pl.multiple_of((c + 2 * qb) * 128, 128), 128)],
            mq.at[n, qb, pl.ds(pl.multiple_of(yh * 512, 512), 512), :],
            own_sem.at[n, qb],
        )

    at_source = z == aux
    events = sorted(((1.5 * j + h, j, h) for j in range(4) for h in range(4)))
    events = [(j, h) for _, j, h in events]

    pl.loop(0, 4)(tree_step)
    phase_e()
    pl.loop(4, 7)(tree_step)
    phase_t()
    pl.loop(7, 10)(tree_step)
    phase_plane()
    for i in range(10, chunks + DEEPEST):
        tree_step(jnp.int32(i))
        for j, h in events[2 * (i - 10):2 * (i - 9)]:
            z_event(j, h)
    for j, h in events[2 * (chunks + DEEPEST - 10):]:
        z_event(j, h)
    for j in range(4):
        t_done(j)

    @pl.when(at_source)
    def _():
        for n in range(nb):
            for qb in range(2):
                own_copy(n, qb).start()
        for n in range(nb):
            for qb in range(2):
                own_copy(n, qb).wait()

    @pl.loop(0, nb)
    def _(n):
        for qb in range(2):
            mqt[n, qb * 128:(qb + 1) * 128, :] = mq[n, qb].T

    def o_copy(j):
        return remote(sbuf.at[j], rbuf.at[j], o_s.at[j], o_r.at[j], partner)

    for j in range(4):
        remote(tbuf.at[j, c], tbuf.at[j, 1 - c], ts_s.at[j], ts_r.at[j], sibling).wait_recv()

        @pl.loop(0, nb)
        def _(n, j=j):
            for core in range(2):
                nt[:, core * 256:(core + 1) * 256] = jnp.dot(
                    mqt[n], tbuf[j, core].reshape(1024, 256), preferred_element_type=F32
                ).astype(BF16)
            part = jnp.dot(nt[...], mp[n], preferred_element_type=F32).reshape(2, 128, 512)

            @pl.when(n == 0)
            def _():
                acc[...] = part

            @pl.when(n > 0)
            def _():
                acc[...] += part

        sbuf[j] = acc[1 - yh].astype(BF16)
        o_copy(j).start()
        out_ref[j] = acc[yh]
    for j in range(4):
        o_copy(j).wait_recv()
        out_ref[j] += rbuf[j].astype(F32)

    @pl.when(c == x // 2)
    def _():
        for copy in g_copies:
            copy.wait_send()

    pl.loop(0, chunks)(tree_sends_done)
    for n in range(nb):
        sib_copy(n).wait_send()
    for d in range(1, 8):
        e_copy(d).wait_send()
        plane_copy(d).wait_send()
    for j in range(4):
        for h in range(hops_up(j)):
            z_copy(j, h, True).wait_send()
        for h in range(hops_down(j)):
            z_copy(j, h, False).wait_send()
        remote(tbuf.at[j, c], tbuf.at[j, c], ts_s.at[j], ts_r.at[j], sibling).wait_send()
        o_copy(j).wait_send()


def per_device(
    three_center,
    block_mask,
    green_functions,
    time_slot,
    grid_times,
    grid_frequencies,
    cosine_weights,
):
    nbatch = three_center.shape[1]
    time_count = time_slot.shape[0]
    cosine_table = cosine_weights * jnp.cos(grid_frequencies[:, None] * grid_times[None, :])
    slot_match = (time_slot[:, None] == jnp.arange(time_count, dtype=jnp.int32)[None, :]).astype(F32)
    pair_coefs = jnp.dot(cosine_table, slot_match.T, precision=lax.Precision.HIGHEST)
    weights = 0.5 * jnp.repeat(pair_coefs, 2, axis=1)
    by_batch = jnp.transpose(three_center, (1, 0, 2))
    dma = pltpu.SemaphoreType.DMA
    vmem = pl.BlockSpec(memory_space=pltpu.VMEM)
    smem = pl.BlockSpec(memory_space=pltpu.SMEM)
    result = pl.pallas_call(
        kernel,
        name="polarizability",
        out_shape=jax.ShapeDtypeStruct((4, 128, 512), F32),
        in_specs=[vmem, smem, vmem, smem],
        out_specs=vmem,
        scratch_shapes=[
            pltpu.VMEM((nbatch, 512, 512), BF16),
            pltpu.VMEM((nbatch, 2, 1024, 128), BF16),
            pltpu.VMEM((nbatch, 256, 1024), BF16),
            pltpu.VMEM((4, 2, 8, 8, 16, 256), BF16),
            pltpu.VMEM((128, 1024), BF16),
            pltpu.VMEM((128, 256), F32),
            pltpu.VMEM((8, 16, 256), F32),
            pltpu.VMEM((4, 16, 256), BF16),
            pltpu.VMEM((256, 512), BF16),
            pltpu.VMEM((2, 128, 512), F32),
            pltpu.VMEM((4, 128, 512), BF16),
            pltpu.VMEM((4, 128, 512), BF16),
            dma((nbatch,)), dma((nbatch,)),
            dma((2,)), dma,
            dma((nbatch, 2)),
            dma((8, 4, 2 * nbatch)), dma((8, 2 * nbatch)),
            dma((7,)), dma((7,)),
            dma((7,)), dma((7,)),
            dma((2, 4, 4)), dma((2, 4, 4)),
            dma((4,)), dma((4,)),
            dma((4,)), dma((4,)),
        ],
        compiler_params=pltpu.CompilerParams(
            collective_id=0, has_side_effects=True, vmem_limit_bytes=48 * 1024 * 1024
        ),
        cost_estimate=pl.CostEstimate(flops=9_700_000_000, bytes_accessed=3_000_000, transcendentals=0),
    )(by_batch, block_mask, green_functions[0], weights)
    return jnp.transpose(result, (1, 0, 2))


def solution(mesh):
    return jax.shard_map(
        per_device,
        mesh=mesh,
        in_specs=(
            P("orb", None, "aux"),
            P("orb", None, "aux"),
            P("tm", "orb", None),
            P(),
            P(),
            P(),
            P(),
        ),
        out_specs=P(("tm", "orb"), None, "aux"),
        check_vma=False,
    )
```

time: 535 us -> 117 us (0.22)
  waiting for transfers between devices: 469 us -> 0 us
  Pallas kernels: 0 us -> 110 us
  matrix products: 22.7 us -> 0.92 us
  between operations: 13.5 us -> 0.01 us
  starting transfers between devices: 11.5 us -> 0 us
  other arithmetic: 11 us -> 0 us
    all_to_all x1 -> x0, waiting for transfers between devices: 186 us -> none  [per_device(): lax.all_to_all(partial_chi, ('tm', 'orb'), split_axis=0, concat_axis=0, t...]
    all_gather x1 -> x0, waiting for transfers between devices: 134 us -> none  [per_device(): lax.all_gather(partner, 'aux', axis=2, tiled=True)]
    reduce_scatter x1 -> x0, waiting for transfers between devices: 115 us -> none  [per_device(): lax.psum_scatter(lax.dot_general(own_green, flat_rows, contract, preferre...]
    pallas_call x0 -> x1, Pallas kernels: none -> 110 us  [per_device(): pl.pallas_call(kernel, name='polarizability', out_shape=jax.ShapeDtypeStr...]
    ppermute x1 -> x0, waiting for transfers between devices: 33.9 us -> none  [from_partner(): lax.ppermute(value, axis, [(i, i ^ 1 << stride) for i in range(lax.axis_s...]
    dot_general x3 -> x0, matrix products: 22.5 us -> none  [the longest x1 12.2 us: pair_term(): lax.dot_general(shard_piece, other_side, (((0, 1), (0, 1)), ((), ())), pr...]
    all_to_all x1 -> x0, starting transfers between devices: 10.2 us -> none  [per_device(): lax.all_to_all(partial_chi, ('tm', 'orb'), split_axis=0, concat_axis=0, t...]
  transfers between devices with their start and end apart: 4 -> 0, of which waited for: 4 -> 0; matrix products, arithmetic and copies ran while one was open for 0% -> 0% of each run, Pallas kernels for 0% -> 0%
where the time goes in v1:
time: 117 us; the launch traced here: 116 us
  Pallas kernels  110 us (94%)
  local copies, waits for them, and re-layouts  5.1 us (4%)
    pallas_call x1, Pallas kernels, per_device(): pl.pallas_call(kernel, name='polarizability', out_shape=jax.ShapeDtypeStr...  110 us
    unnamed x5, local copies, waits for them, and re-layouts  3.27 us

profile of v1, /device:TPU:1, one launch (start us, length us, event | category | flops | bytes accessed | tf_op | source)
XLA Modules:
  0.0 115.9 jit_solution(7674024453758119900)
XLA Ops:
  0.0 0.9 convolution_multiply_fusion
  0.9 0.1 copy.8
  1.0 0.1 copy.10.w_ref
  1.1 0.8 copy.9.mask_ref
  1.9 0.0 copy-start
  1.9 1.4 %copy-done = bf16[256,6,512]{2,0,1:T(8,128)(2,1)S(1)} copy-done((bf16[256,6,512]{2,0,1:T(8,128)(2,1)S(1)}, bf16[256,6,512]{2,0,1:T(8,128)(2,1)}, u32[]{:S(2)}) %copy-start) | copy-done | bytes 1572888
  3.3 0.0 copy-start.1
  3.3 1.0 copy-done.1
  4.4 109.8 %polarizability.1 = f32[4,128,512]{2,1,0:T(8,128)S(1)} custom-call(bf16[6,256,512]{2,1,0:T(8,128)(2,1)S(1)} %bitcast.5, s32[4,6,4]{2,1,0:T(8,128)S(1)} %copy.9.mask_ref, bf16[256,1024]{1,0:T(8,128)(2,1)S(1)} %bitcast.6, f32[4,8]{1,0:T(4,128)S(1)} %copy.10.w_ref), custom_call_target="tpu_custom_call" | custom-call | flops 9699999744 | bytes 3000000 | tf_op jit(solution)/shard_map/polarizability/pallas_call | solution.py:303
  114.2 1.6 %copy.11 = f32[128,4,512]{2,1,0:T(4,128)} copy(f32[128,4,512]{2,0,1:T(8,128)S(1)} %bitcast.4) | data formatting | bytes 2097152 | tf_op jit(solution)/shard_map/transpose | solution.py:337
  (1 shorter events, 0.0 us)
Async XLA Ops:
  1.9 1.4 %copy-start = (bf16[256,6,512]{2,0,1:T(8,128)(2,1)S(1)}, bf16[256,6,512]{2,0,1:T(8,128)(2,1)}, u32[]{:S(2)}) copy-start(bf16[256,6,512]{2,0,1:T(8,128)(2,1)} %param.7) | copy-start | bytes 4718596
  3.3 1.0 copy-start.1

commit v2 on v0

v2 whole, which is shorter than its diff:
```python
import jax
import jax.numpy as jnp
from jax import lax
from jax.experimental import pallas as pl
from jax.experimental.pallas import tpu as pltpu
from jax.sharding import PartitionSpec as P

MESH = pl.DeviceIdType.MESH
F32 = jnp.float32
BF16 = jnp.bfloat16
PARTS = 2


def kernel(
    m_ref, mask_ref, g_ref, w_ref, out_ref,
    mp, mq, mqt, sbuf, gc, es, er, smy, nt, acc, own, oout, oin,
    sib_s, sib_r, g_s, g_r, e_s, e_r, sc_s, sc_r, p1_s, p1_r, p2_s, p2_r, pl_s, pl_r, z_s, z_r, t_s, t_r, o_s, o_r,
):
    nb = m_ref.shape[0]
    z = lax.axis_index("tm")
    orb = lax.axis_index("orb")
    aux = lax.axis_index("aux")
    yh, c = orb // 2, orb % 2
    yl, x = aux // 4, aux % 4
    y = 2 * yh + yl

    def dev(to_x, to_y, to_z, core):
        return (to_z, (to_y // 2) * 2 + core, (to_y % 2) * 4 + to_x)

    def remote(src, dst, s, r, where):
        return pltpu.make_async_remote_copy(
            src_ref=src, dst_ref=dst, send_sem=s, recv_sem=r, device_id=where, device_id_type=MESH
        )

    def rows(start, size):
        return pl.ds(pl.multiple_of(start, size), size)

    sibling = (z, yh * 2 + 1 - c, aux)
    partner = (z, (1 - yh) * 2 + c, aux)
    zpair = z + 1 - 2 * (z % 2)
    swapped = [(zpair, yl * 2 + core, yh * 4 + x) for core in range(2)]
    z_next = ((z + 1) % 8, orb, aux)
    z_last = ((z + 7) % 8, orb, aux)
    i = (x + 4 - z % 4) % 4
    el = (y + 4 - z // 4) % 4
    place = el * 4 + i
    x_peers = [dev((x + d) % 4, y, z, c) for d in range(1, 4)]
    y_peers = [dev(x, (y + d) % 4, z, c) for d in range(1, 4)]

    barrier = pltpu.get_barrier_semaphore()
    greet = [sibling] + swapped + x_peers + y_peers + [z_next, z_last]
    greet += [dev((x + d) % 4, yh * 2 + 1 - yl, z, c) for d in range(1, 4)]
    for where in greet:
        pl.semaphore_signal(barrier, inc=1, device_id=where, device_id_type=MESH)
    for d in range(8):
        pl.semaphore_signal(barrier, inc=1, device_id=((z + d) % 8, el, z), device_id_type=MESH)

    for n in range(nb):
        for b in range(4):
            for ab in range(4):
                present = jnp.full((64, 128), mask_ref[b, n, ab].astype(F32), F32).astype(BF16)
                mp[n, rows(c * 256 + b * 64, 64), ab * 128:(ab + 1) * 128] = (
                    m_ref[n, b * 64:(b + 1) * 64, ab * 128:(ab + 1) * 128] * present
                )
    pl.semaphore_wait(barrier, len(greet) + 8)

    half_rows = rows((x % 2) * 128, 128)

    def g_copy(core):
        return remote(g_ref.at[half_rows, :], gc, g_s.at[core], g_r, swapped[core])

    @pl.when(c == x // 2)
    def _():
        for core in range(2):
            g_copy(core).start()

    strip = (z // 2) * 16

    def scatter(step, core):
        src = mp.at[:, rows(c * 256 + step * 64 + strip, 16), rows((core + 2 * (z % 2)) * 128, 128)]
        dst = mq.at[:, z % 2, orb, step, rows(strip, 16), :]
        where = dev((x + step) % 4, (y + c) % 4, aux, core)
        return src, dst, where

    def scatter_all(act):
        for step in range(4):
            for core in range(2):
                src, dst, where = scatter(step, core)
                send = remote(src, dst, sc_s.at[step, core], sc_r.at[z], where)
                if step == 0 and core == 0:
                    to_self = (z == aux) & (c == 0)

                    @pl.when(to_self)
                    def _():
                        if act == "start":
                            pltpu.make_async_copy(src, dst, sc_r.at[z]).start()

                    @pl.when(jnp.logical_not(to_self))
                    def _():
                        if act == "start":
                            send.start()
                        else:
                            send.wait_send()
                elif act == "start":
                    send.start()
                else:
                    send.wait_send()

    scatter_all("start")

    def sib_copy(n):
        mine = rows(c * 256, 256)
        part = pl.ds(n * 3, 3)
        return remote(mp.at[part, mine, :], mp.at[part, mine, :], sib_s.at[n], sib_r.at[n], sibling)

    for n in range(PARTS):
        sib_copy(n).start()

    keep = z % 2

    def e_copy():
        return remote(es.at[1 - keep], er, e_s, e_r, (zpair, orb, aux))

    def plane_copy(d):
        return remote(smy, sbuf.at[z, c, aux], pl_s.at[d - 1], pl_r.at[d - 1], (z, orb, (aux + d) % 8))

    g_copy(0).wait_recv()
    es[...] = (0.5 * lax.dot_general(
        gc[...], g_ref[...], (((1,), (1,)), ((), ())), preferred_element_type=F32
    )).reshape(2, 64, 256)
    e_copy().start()

    def first_copy(part, way, d):
        span = pl.ds(part * 3, 3)
        piece = mq.at[span, way, el, i]
        peer = (x_peers if way == 0 else y_peers)[d]
        return remote(piece, piece, p1_s.at[part, way, d], p1_r.at[part, way, d], peer)

    def second_copy(part, way, d):
        span = pl.ds(part * 3, 3)
        piece = mq.at[span, 0, el] if way == 0 else mq.at[span, 1, :, i]
        peer = (y_peers if way == 0 else x_peers)[d]
        return remote(piece, piece, p2_s.at[part, way, d], p2_r.at[part, way, d], peer)

    for s in range(8):
        src, dst, where = scatter(1, 0)
        remote(src, dst, sc_s.at[1, 0], sc_r.at[s], where).wait_recv()
    for part in range(PARTS):
        for way in range(2):
            for d in range(3):
                first_copy(part, way, d).start()

    e_copy().wait_recv()
    smy[...] = (es[keep] + er[...]).astype(BF16)
    for d in range(1, 8):
        plane_copy(d).start()
    sbuf[z, c, aux] = smy[...]

    for part in range(PARTS):
        for way in range(2):
            for d in range(3):
                first_copy(part, way, d).wait_recv()
            for d in range(3):
                second_copy(part, way, d).start()

    def z_copy(h, half, up):
        origin = (z + 8 - h) % 8 if up else (z + h) % 8
        piece = sbuf.at[origin, c, pl.ds(half * 4, 4)]
        way = 0 if up else 1
        return remote(piece, piece, z_s.at[way, half, h], z_r.at[way, half, h], z_next if up else z_last)

    def hops(half, up):
        return 4 if (half == 0) == up else 3

    def to_sibling(h, half, up):
        origin = (z + 8 - h) % 8 if up else (z + h) % 8
        piece = sbuf.at[origin, c, pl.ds(half * 4, 4)]
        way = 0 if up else 1
        return remote(piece, piece, t_s.at[way, half, h], t_r.at[way, half, h], sibling)

    WAYS = [(half, up) for half in range(2) for up in (True, False)]

    def z_event(h):
        for half, up in WAYS:
            if h <= hops(half, up):
                if h > 0:
                    z_copy(h - 1, half, up).wait_recv()
                if h < hops(half, up):
                    z_copy(h, half, up).start()
                if h > 0 or up:
                    to_sibling(h, half, up).start()

    def sibling_ready(h):
        for half, up in WAYS:
            if h <= hops(half, up) and (h > 0 or up):
                to_sibling(h, half, up).wait_recv()

    for d in range(1, 8):
        plane_copy(d).wait_recv()
    z_event(0)
    z_event(1)
    z_event(2)

    for n in range(PARTS):
        sib_copy(n).wait_recv()
    for part in range(PARTS):
        for way in range(2):
            for d in range(3):
                second_copy(part, way, d).wait_recv()

        @pl.loop(part * 3, part * 3 + 3)
        def _(n):
            for qb in range(2):
                block = mq[n, qb].reshape(8, 2, 64, 128)
                for half in range(2):
                    mqt[n, half, qb * 128:(qb + 1) * 128, :] = block[:, half].reshape(512, 128).T

    turn = 1 - 2 * (z % 2)
    order = [z // 2, (z // 2 + 4 - turn) % 4, (z // 2 + 4 + turn) % 4, (z // 2 + 2) % 4]

    def o_copy(r):
        return remote(oout.at[r], oin.at[r], o_s.at[r], o_r.at[r], partner)

    sibling_ready(0)
    for r in range(4):
        if r >= 2:
            z_event(r + 1)
        sibling_ready(r + 1)

        @pl.loop(0, nb)
        def _(n, r=r):
            for core in range(2):
                nt[:, core * 256:(core + 1) * 256] = (
                    jnp.dot(mqt[n, 0], sbuf[2 * order[r], core].reshape(512, 256), preferred_element_type=F32)
                    + jnp.dot(mqt[n, 1], sbuf[2 * order[r] + 1, core].reshape(512, 256), preferred_element_type=F32)
                ).astype(BF16)
            part = jnp.dot(nt[...], mp[n], preferred_element_type=F32).reshape(2, 128, 512)

            @pl.when(n == 0)
            def _():
                acc[...] = part

            @pl.when(n > 0)
            def _():
                acc[...] += part

        oout[r] = acc[1 - yh].astype(BF16)
        o_copy(r).start()
        own[r] = acc[yh]
    for r in range(4):
        o_copy(r).wait_recv()
        whole = own[r] + oin[r].astype(F32)
        for j in range(4):
            if r == 0:
                out_ref[j] = w_ref[j, order[r]] * whole
            else:
                out_ref[j] += w_ref[j, order[r]] * whole

    @pl.when(c == x // 2)
    def _():
        for core in range(2):
            g_copy(core).wait_send()

    scatter_all("wait")
    for n in range(PARTS):
        sib_copy(n).wait_send()
        for way in range(2):
            for d in range(3):
                first_copy(n, way, d).wait_send()
                second_copy(n, way, d).wait_send()
    e_copy().wait_send()
    for d in range(1, 8):
        plane_copy(d).wait_send()
    for half, up in WAYS:
        for h in range(hops(half, up) + 1):
            if h < hops(half, up):
                z_copy(h, half, up).wait_send()
            if h > 0 or up:
                to_sibling(h, half, up).wait_send()
    for r in range(4):
        o_copy(r).wait_send()


def per_device(
    three_center,
    block_mask,
    green_functions,
    time_slot,
    grid_times,
    grid_frequencies,
    cosine_weights,
):
    nb = three_center.shape[1]
    time_count = time_slot.shape[0]
    cosine_table = cosine_weights * jnp.cos(grid_frequencies[:, None] * grid_times[None, :])
    slot_match = (time_slot[:, None] == jnp.arange(time_count, dtype=jnp.int32)[None, :]).astype(F32)
    pair_coefs = jnp.dot(cosine_table, slot_match.T, precision=lax.Precision.HIGHEST)
    by_batch = jnp.transpose(three_center, (1, 0, 2))
    dma = pltpu.SemaphoreType.DMA
    vmem = pl.BlockSpec(memory_space=pltpu.VMEM)
    smem = pl.BlockSpec(memory_space=pltpu.SMEM)
    result = pl.pallas_call(
        kernel,
        name="polarizability",
        out_shape=jax.ShapeDtypeStruct((4, 128, 512), F32),
        in_specs=[vmem, smem, vmem, smem],
        out_specs=vmem,
        scratch_shapes=[
            pltpu.VMEM((nb, 512, 512), BF16),
            pltpu.VMEM((nb, 2, 4, 4, 64, 128), BF16),
            pltpu.VMEM((nb, 2, 256, 512), BF16),
            pltpu.VMEM((8, 2, 8, 64, 256), BF16),
            pltpu.VMEM((128, 1024), BF16),
            pltpu.VMEM((2, 64, 256), F32),
            pltpu.VMEM((64, 256), F32),
            pltpu.VMEM((64, 256), BF16),
            pltpu.VMEM((256, 512), BF16),
            pltpu.VMEM((2, 128, 512), F32),
            pltpu.VMEM((4, 128, 512), F32),
            pltpu.VMEM((4, 128, 512), BF16),
            pltpu.VMEM((4, 128, 512), BF16),
            dma((PARTS,)), dma((PARTS,)),
            dma((2,)), dma,
            dma, dma,
            dma((4, 2)), dma((8,)),
            dma((PARTS, 2, 3)), dma((PARTS, 2, 3)),
            dma((PARTS, 2, 3)), dma((PARTS, 2, 3)),
            dma((7,)), dma((7,)),
            dma((2, 2, 4)), dma((2, 2, 4)),
            dma((2, 2, 5)), dma((2, 2, 5)),
            dma((4,)), dma((4,)),
        ],
        compiler_params=pltpu.CompilerParams(
            collective_id=0, has_side_effects=True, vmem_limit_bytes=48 * 1024 * 1024
        ),
        cost_estimate=pl.CostEstimate(flops=9_700_000_000, bytes_accessed=3_000_000, transcendentals=0),
    )(by_batch, block_mask, green_functions[0], pair_coefs)
    return jnp.transpose(result, (1, 0, 2))


def solution(mesh):
    return jax.shard_map(
        per_device,
        mesh=mesh,
        in_specs=(
            P("orb", None, "aux"),
            P("orb", None, "aux"),
            P("tm", "orb", None),
            P(),
            P(),
            P(),
            P(),
        ),
        out_specs=P(("tm", "orb"), None, "aux"),
        check_vma=False,
    )
```

time: 535 us -> 93.6 us (0.17)
  waiting for transfers between devices: 469 us -> 0 us
  Pallas kernels: 0 us -> 87.6 us
  matrix products: 22.7 us -> 0.92 us
  between operations: 13.5 us -> 0.01 us
  starting transfers between devices: 11.5 us -> 0 us
  other arithmetic: 11 us -> 0 us
    all_to_all x1 -> x0, waiting for transfers between devices: 186 us -> none  [per_device(): lax.all_to_all(partial_chi, ('tm', 'orb'), split_axis=0, concat_axis=0, t...]
    all_gather x1 -> x0, waiting for transfers between devices: 134 us -> none  [per_device(): lax.all_gather(partner, 'aux', axis=2, tiled=True)]
    reduce_scatter x1 -> x0, waiting for transfers between devices: 115 us -> none  [per_device(): lax.psum_scatter(lax.dot_general(own_green, flat_rows, contract, preferre...]
    pallas_call x0 -> x1, Pallas kernels: none -> 87.6 us  [per_device(): pl.pallas_call(kernel, name='polarizability', out_shape=jax.ShapeDtypeStr...]
    ppermute x1 -> x0, waiting for transfers between devices: 33.9 us -> none  [from_partner(): lax.ppermute(value, axis, [(i, i ^ 1 << stride) for i in range(lax.axis_s...]
    dot_general x3 -> x0, matrix products: 22.5 us -> none  [the longest x1 12.2 us: pair_term(): lax.dot_general(shard_piece, other_side, (((0, 1), (0, 1)), ((), ())), pr...]
    all_to_all x1 -> x0, starting transfers between devices: 10.2 us -> none  [per_device(): lax.all_to_all(partial_chi, ('tm', 'orb'), split_axis=0, concat_axis=0, t...]
  transfers between devices with their start and end apart: 4 -> 0, of which waited for: 4 -> 0; matrix products, arithmetic and copies ran while one was open for 0% -> 0% of each run, Pallas kernels for 0% -> 0%
where the time goes in v2:
time: 93.6 us; the launch traced here: 93.4 us
  Pallas kernels  87.6 us (94%)
  local copies, waits for them, and re-layouts  4.91 us (5%)
    pallas_call x1, Pallas kernels, per_device(): pl.pallas_call(kernel, name='polarizability', out_shape=jax.ShapeDtypeStr...  87.6 us
    unnamed x5, local copies, waits for them, and re-layouts  3.27 us

profile of v2, /device:TPU:1, one launch (start us, length us, event | category | flops | bytes accessed | tf_op | source)
XLA Modules:
  0.0 93.4 jit_solution(8685624462004882630)
XLA Ops:
  0.0 0.9 fusion.w_ref
  0.9 0.8 copy.8.mask_ref
  1.7 0.0 copy-start
  1.7 1.4 %copy-done = bf16[256,6,512]{2,0,1:T(8,128)(2,1)S(1)} copy-done((bf16[256,6,512]{2,0,1:T(8,128)(2,1)S(1)}, bf16[256,6,512]{2,0,1:T(8,128)(2,1)}, u32[]{:S(2)}) %copy-start) | copy-done | bytes 1572888
  3.2 0.0 copy-start.1
  3.2 1.0 %copy-done.1 = bf16[1,256,1024]{2,1,0:T(8,128)(2,1)S(1)} copy-done((bf16[1,256,1024]{2,1,0:T(8,128)(2,1)S(1)}, bf16[1,256,1024]{2,1,0:T(8,128)(2,1)}, u32[]{:S(2)}) %copy-start.1) | copy-done | bytes 524312
  4.2 87.6 %polarizability.1 = f32[4,128,512]{2,1,0:T(8,128)S(1)} custom-call(bf16[6,256,512]{2,1,0:T(8,128)(2,1)S(1)} %bitcast.4, s32[4,6,4]{2,1,0:T(8,128)S(1)} %copy.8.mask_ref, bf16[256,1024]{1,0:T(8,128)(2,1)S(1)} %bitcast.5, f32[4,4]{1,0:T(4,128)S(1)} %fusion.w_ref), custom_call_target="tpu_custom_call" | custom-call | flops 9699999744 | bytes 3000000 | tf_op jit(solution)/shard_map/polarizability/pallas_call | solution.py:302
  91.8 1.6 %copy.9 = f32[128,4,512]{2,1,0:T(4,128)} copy(f32[128,4,512]{2,0,1:T(8,128)S(1)} %bitcast.3) | data formatting | bytes 2097152 | tf_op jit(solution)/shard_map/transpose | solution.py:338
Async XLA Ops:
  1.7 1.4 %copy-start = (bf16[256,6,512]{2,0,1:T(8,128)(2,1)S(1)}, bf16[256,6,512]{2,0,1:T(8,128)(2,1)}, u32[]{:S(2)}) copy-start(bf16[256,6,512]{2,0,1:T(8,128)(2,1)} %param.7) | copy-start | bytes 4718596
  3.2 1.0 %copy-start.1 = (bf16[1,256,1024]{2,1,0:T(8,128)(2,1)S(1)}, bf16[1,256,1024]{2,1,0:T(8,128)(2,1)}, u32[]{:S(2)}) copy-start(bf16[1,256,1024]{2,1,0:T(8,128)(2,1)} %param.9) | copy-start | bytes 1572868

commit v3 on v2

v3 whole, which is shorter than its diff:
```python
import jax
import jax.numpy as jnp
from jax import lax
from jax.experimental import pallas as pl
from jax.experimental.pallas import tpu as pltpu
from jax.sharding import PartitionSpec as P

MESH = pl.DeviceIdType.MESH
F32 = jnp.float32
BF16 = jnp.bfloat16
PARTS = 3


def kernel(
    m_ref, g_ref, mask_ref, slot_ref, time_ref, freq_ref, cw_ref, out_ref,
    m_in, g_in, mp, stage, mq, mqt, sbuf, gc, es, er, smy, nt, own, oout, oin,
    in_sem, sib_s, sib_r, g_s, g_r, e_s, e_r, sp_s, sp_r, sc_s, sc_r, p1_s, p1_r, p2_s, p2_r, pl_s, pl_r, z_s, z_r, t_s, t_r, o_s, o_r,
):
    nb = m_ref.shape[0]
    load_m = pltpu.make_async_copy(m_ref, m_in, in_sem.at[0])
    load_g = pltpu.make_async_copy(g_ref, g_in, in_sem.at[1])
    load_m.start()
    load_g.start()
    z = lax.axis_index("tm")
    orb = lax.axis_index("orb")
    aux = lax.axis_index("aux")
    yh, c = (orb >> 1), (orb & 1)
    yl, x = (aux >> 2), (aux & 3)
    y = 2 * yh + yl

    def dev(to_x, to_y, to_z, core):
        return (to_z, ((to_y >> 1)) * 2 + core, ((to_y & 1)) * 4 + to_x)

    def remote(src, dst, s, r, where):
        return pltpu.make_async_remote_copy(
            src_ref=src, dst_ref=dst, send_sem=s, recv_sem=r, device_id=where, device_id_type=MESH
        )

    def rows(start, size):
        return pl.ds(pl.multiple_of(start, size), size)

    sibling = (z, yh * 2 + 1 - c, aux)
    partner = (z, (1 - yh) * 2 + c, aux)
    zpair = z + 1 - 2 * ((z & 1))
    swapped = [(zpair, yl * 2 + core, yh * 4 + x) for core in range(2)]
    z_next = ((z + 1) & 7, orb, aux)
    z_last = ((z + 7) & 7, orb, aux)
    i = (x + 4 - (z & 3)) & 3
    el = (y + 4 - (z >> 2)) & 3
    place = el * 4 + i
    x_peers = [dev((x + d) & 3, y, z, c) for d in range(1, 4)]
    y_peers = [dev(x, (y + d) & 3, z, c) for d in range(1, 4)]

    barrier = pltpu.get_barrier_semaphore()
    greet = [sibling] + swapped + x_peers + y_peers + [z_next, z_last]
    greet += [dev((x + d) & 3, yh * 2 + 1 - yl, z, c) for d in range(1, 4)]
    greet += [((z + d) & 7, orb, aux) for d in (2, 3, 5, 6)]
    greet += [(z, (y + 4 - (slab >> 2)) & 3, slab) for slab in range(8)]
    for where in greet:
        pl.semaphore_signal(barrier, inc=1, device_id=where, device_id_type=MESH)

    load_m.wait()
    for n in range(nb):
        for b in range(4):
            for ab in range(4):
                present = jnp.full((64, 128), mask_ref[b, ab, n].astype(F32), F32).astype(BF16)
                mp[n, rows(c * 256 + b * 64, 64), ab * 128:(ab + 1) * 128] = (
                    m_in[n, b * 64:(b + 1) * 64, ab * 128:(ab + 1) * 128] * present
                )
    pl.semaphore_wait(barrier, len(greet))

    half_rows = rows(((x & 1)) * 128, 128)

    def g_copy(core):
        return remote(g_ref.at[half_rows, :], gc, g_s.at[core], g_r, swapped[core])

    @pl.when(c == (x >> 1))
    def _():
        for core in range(2):
            g_copy(core).start()

    ahead = (z + 8 - aux) & 7
    batch = jnp.where(ahead == 0, 0, jnp.where(ahead < 4, 2 * ahead - 1, 2 * (8 - ahead)))
    batch = jnp.minimum(batch, nb - 1)

    def spread(step, core, qb):
        src = mp.at[batch, rows(c * 256 + step * 64, 64), rows((core + 2 * qb) * 128, 128)]
        dst = stage.at[ahead, qb]
        where = dev((x + step) & 3, (y + c) & 3, z, core)
        return src, dst, where

    def spread_all(act):
        for qb in range(2):
            sends = (ahead < 3) | (ahead > 5) | ((ahead == 3) if qb == 0 else (ahead == 5))

            @pl.when(sends)
            def _(qb=qb):
                for step in range(4):
                    for core in range(2):
                        src, dst, where = spread(step, core, qb)
                        send = remote(src, dst, sp_s.at[step, core, qb], sp_r.at[ahead, qb], where)

                        def go(send=send):
                            if act == "start":
                                send.start()
                            else:
                                send.wait_send()

                        if step == 0 and core == 0:
                            pl.when(c == 1)(go)
                            if act == "start":
                                @pl.when(c == 0)
                                def _():
                                    pltpu.make_async_copy(src, dst, sp_r.at[ahead, qb]).start()
                        else:
                            go()

    spread_all("start")

    def behind(dz, qb):
        slab = (z + 8 - dz) & 7
        n = 0 if dz == 0 else (2 * dz - 1 if dz < 4 else 2 * (8 - dz))
        n = min(n, nb - 1)
        dst = mq.at[n, qb, (y + 4 - (slab >> 2)) & 3, (x + 4 - (slab & 3)) & 3]
        if dz == 0:
            return pltpu.make_async_copy(stage.at[dz, qb], dst, sc_r.at[n, qb])
        return remote(stage.at[dz, qb], dst, sc_s.at[dz, qb], sc_r.at[n, qb], (slab, orb, aux))

    BLOCKS = [(dz, qb) for dz in (0, 1, 7, 2, 6) for qb in range(2)] + [(3, 0), (5, 1)]

    def pass_on():
        for dz, qb in BLOCKS:
            remote(stage.at[dz, qb], stage.at[dz, qb], sp_s.at[0, 0, qb], sp_r.at[dz, qb], sibling).wait_recv()
            behind(dz, qb).start()

    def sib_copy(n):
        mine = rows(c * 256, 256)
        part = pl.ds(n * 2, 2)
        return remote(mp.at[part, mine, :], mp.at[part, mine, :], sib_s.at[n], sib_r.at[n], sibling)

    for n in range(PARTS):
        sib_copy(n).start()

    keep = (z & 1)

    def e_copy():
        return remote(es.at[1 - keep], er, e_s, e_r, (zpair, orb, aux))

    def plane_copy(d):
        return remote(smy, sbuf.at[z, c, aux], pl_s.at[d - 1], pl_r.at[d - 1], (z, orb, (aux + d) & 7))


    def first_copy(part, way, d):
        span = pl.ds(part * 2, 2)
        piece = mq.at[span, way, el, i]
        peer = (x_peers if way == 0 else y_peers)[d]
        return remote(piece, piece, p1_s.at[part, way, d], p1_r.at[part, way, d], peer)

    def second_copy(part, way, d):
        span = pl.ds(part * 2, 2)
        piece = mq.at[span, 0, el] if way == 0 else mq.at[span, 1, :, i]
        peer = (y_peers if way == 0 else x_peers)[d]
        return remote(piece, piece, p2_s.at[part, way, d], p2_r.at[part, way, d], peer)

    def first(part):
        for n in (2 * part, 2 * part + 1):
            for qb in range(2):
                remote(mq.at[n, qb, 0, 0], mq.at[n, qb, 0, 0], sc_s.at[1, qb], sc_r.at[n, qb], sibling).wait_recv()
        for way in range(2):
            for d in range(3):
                first_copy(part, way, d).start()

    def second(part):
        for way in range(2):
            for d in range(3):
                first_copy(part, way, d).wait_recv()
            for d in range(3):
                second_copy(part, way, d).start()

    def second_done(part):
        for way in range(2):
            for d in range(3):
                second_copy(part, way, d).wait_recv()

        @pl.loop(part * 2, part * 2 + 2)
        def _(n):
            for qb in range(2):
                block = mq[n, qb].reshape(8, 2, 64, 128)
                for half in range(2):
                    mqt[n, qb * 128:(qb + 1) * 128, half * 512:(half + 1) * 512] = (
                        block[:, half].reshape(512, 128).T
                    )

    def z_copy(h, half, up):
        origin = (z + 8 - h) & 7 if up else (z + h) & 7
        piece = sbuf.at[origin, c, pl.ds(half * 4, 4)]
        way = 0 if up else 1
        return remote(piece, piece, z_s.at[way, half, h], z_r.at[way, half, h], z_next if up else z_last)

    def hops(half, up):
        return 4 if (half == 0) == up else 3

    def to_sibling(h, half, up):
        origin = (z + 8 - h) & 7 if up else (z + h) & 7
        piece = sbuf.at[origin, c, pl.ds(half * 4, 4)]
        way = 0 if up else 1
        return remote(piece, piece, t_s.at[way, half, h], t_r.at[way, half, h], sibling)

    WAYS = [(half, up) for half in range(2) for up in (True, False)]

    def z_event(h):
        for half, up in WAYS:
            if h <= hops(half, up):
                if h > 0:
                    z_copy(h - 1, half, up).wait_recv()
                if h < hops(half, up):
                    z_copy(h, half, up).start()
                if h > 0 or up:
                    to_sibling(h, half, up).start()

    def sibling_ready(h):
        for half, up in WAYS:
            if h <= hops(half, up) and (h > 0 or up):
                to_sibling(h, half, up).wait_recv()

    turn = 1 - 2 * ((z & 1))
    order = [(z >> 1), ((z >> 1) + 4 - turn) & 3, ((z >> 1) + 4 + turn) & 3, ((z >> 1) + 2) & 3]

    def o_copy(r, side):
        return remote(oout.at[r, side], oin.at[r, side], o_s.at[r, side], o_r.at[r, side], partner)

    def product(r, part):
        batches = slice(part * 2, part * 2 + 2)
        left = mqt[batches].reshape(512, 1024)
        for core in range(2):
            pair = sbuf[pl.ds(2 * order[r], 2), core].reshape(1024, 256)
            nt[:, :, core * 256:(core + 1) * 256] = (
                jnp.dot(left, pair, preferred_element_type=F32).astype(BF16).reshape(2, 256, 256)
            )
        for side in range(2):
            cols = slice(side * 256, (side + 1) * 256)
            total = jnp.dot(nt[0], mp[part * 2, :, cols], preferred_element_type=F32)
            total += jnp.dot(nt[1], mp[part * 2 + 1, :, cols], preferred_element_type=F32)
            total = total.reshape(2, 128, 256)
            if part > 0:
                total += own[r, side]
            own[r, side] = total
            if part == PARTS - 1:
                oout[r, side] = own[r, side, 1 - yh].astype(BF16)
                o_copy(r, side).start()

    def coefs(r):
        slot = slot_ref[order[r]]
        picked = []
        for j in range(4):
            total = jnp.zeros((8, 256), F32)
            for s in range(4):
                total = total + jnp.where(slot == s, table[j][s], 0.0)
            picked.append(total)
        return picked

    def add(r):
        picked = coefs(r)
        for side in range(2):
            o_copy(r, side).wait_recv()
            whole = (own[r, side, yh] + oin[r, side].astype(F32)).reshape(16, 8, 256)
            cols = slice(side * 256, (side + 1) * 256)
            for j in range(4):
                term = (picked[j] * whole).reshape(128, 256)
                if r == 0:
                    out_ref[j, :, cols] = term
                else:
                    out_ref[j, :, cols] += term

    pass_on()
    load_g.wait()
    g_copy(0).wait_recv()
    es[...] = (0.5 * lax.dot_general(
        gc[...], g_in[...], (((1,), (1,)), ((), ())), preferred_element_type=F32
    )).reshape(2, 64, 256)
    e_copy().start()

    e_copy().wait_recv()
    smy[...] = (es[keep] + er[...]).astype(BF16)
    for d in range(1, 8):
        plane_copy(d).start()
    sbuf[z, c, aux] = smy[...]
    table = [
        [cw_ref[j, s] * jnp.cos(jnp.full((8, 256), freq_ref[j] * time_ref[s], F32)) for s in range(4)]
        for j in range(4)
    ]
    first(0)
    first(1)
    first(2)
    for d in range(1, 8):
        plane_copy(d).wait_recv()
    z_event(0)
    second(0)
    z_event(1)
    second(1)
    second(2)
    for n in range(PARTS):
        sib_copy(n).wait_recv()
    z_event(2)
    sibling_ready(0)
    sibling_ready(1)
    second_done(0)
    product(0, 0)
    sibling_ready(2)
    product(1, 0)
    z_event(3)
    second_done(1)
    product(0, 1)
    product(1, 1)
    sibling_ready(3)
    product(2, 0)
    product(2, 1)
    z_event(4)
    sibling_ready(4)
    product(3, 0)
    product(3, 1)
    second_done(2)
    for r in range(4):
        product(r, 2)
    for r in range(4):
        add(r)

    @pl.when(c == (x >> 1))
    def _():
        for core in range(2):
            g_copy(core).wait_send()

    spread_all("wait")
    for dz, qb in BLOCKS:
        if dz > 0:
            behind(dz, qb).wait_send()
    for n in range(PARTS):
        sib_copy(n).wait_send()
        for way in range(2):
            for d in range(3):
                first_copy(n, way, d).wait_send()
                second_copy(n, way, d).wait_send()
    e_copy().wait_send()
    for d in range(1, 8):
        plane_copy(d).wait_send()
    for half, up in WAYS:
        for h in range(hops(half, up) + 1):
            if h < hops(half, up):
                z_copy(h, half, up).wait_send()
            if h > 0 or up:
                to_sibling(h, half, up).wait_send()
    for r in range(4):
        for side in range(2):
            o_copy(r, side).wait_send()


def per_device(
    three_center,
    block_mask,
    green_functions,
    time_slot,
    grid_times,
    grid_frequencies,
    cosine_weights,
):
    nb = three_center.shape[1]
    by_batch = jnp.transpose(three_center, (1, 0, 2))
    dma = pltpu.SemaphoreType.DMA
    vmem = pl.BlockSpec(memory_space=pltpu.VMEM)
    smem = pl.BlockSpec(memory_space=pltpu.SMEM)
    hbm = pl.BlockSpec(memory_space=pl.ANY)
    result = pl.pallas_call(
        kernel,
        name="polarizability",
        out_shape=jax.ShapeDtypeStruct((4, 128, 512), F32),
        in_specs=[hbm, hbm, smem, smem, smem, smem, smem],
        out_specs=vmem,
        scratch_shapes=[
            pltpu.VMEM((nb, 256, 512), BF16),
            pltpu.VMEM((256, 1024), BF16),
            pltpu.VMEM((nb, 512, 512), BF16),
            pltpu.VMEM((8, 2, 64, 128), BF16),
            pltpu.VMEM((nb, 2, 4, 4, 64, 128), BF16),
            pltpu.VMEM((nb, 256, 1024), BF16),
            pltpu.VMEM((8, 2, 8, 64, 256), BF16),
            pltpu.VMEM((128, 1024), BF16),
            pltpu.VMEM((2, 64, 256), F32),
            pltpu.VMEM((64, 256), F32),
            pltpu.VMEM((64, 256), BF16),
            pltpu.VMEM((2, 256, 512), BF16),
            pltpu.VMEM((4, 2, 2, 128, 256), F32),
            pltpu.VMEM((4, 2, 128, 256), BF16),
            pltpu.VMEM((4, 2, 128, 256), BF16),
            dma((2,)),
            dma((PARTS,)), dma((PARTS,)),
            dma((2,)), dma,
            dma, dma,
            dma((4, 2, 2)), dma((8, 2)),
            dma((8, 2)), dma((nb, 2)),
            dma((PARTS, 2, 3)), dma((PARTS, 2, 3)),
            dma((PARTS, 2, 3)), dma((PARTS, 2, 3)),
            dma((7,)), dma((7,)),
            dma((2, 2, 4)), dma((2, 2, 4)),
            dma((2, 2, 5)), dma((2, 2, 5)),
            dma((4, 2)), dma((4, 2)),
        ],
        compiler_params=pltpu.CompilerParams(
            collective_id=0, has_side_effects=True, vmem_limit_bytes=60 * 1024 * 1024
        ),
        cost_estimate=pl.CostEstimate(flops=9_700_000_000, bytes_accessed=3_000_000, transcendentals=0),
    )(
        by_batch, green_functions[0], jnp.transpose(block_mask, (0, 2, 1)),
        time_slot, grid_times, grid_frequencies, cosine_weights,
    )
    return jnp.transpose(result, (1, 0, 2))


def solution(mesh):
    return jax.shard_map(
        per_device,
        mesh=mesh,
        in_specs=(
            P("orb", None, "aux"),
            P("orb", None, "aux"),
            P("tm", "orb", None),
            P(),
            P(),
            P(),
            P(),
        ),
        out_specs=P(("tm", "orb"), None, "aux"),
        check_vma=False,
    )
```

time: 93.6 us -> 77.2 us (0.82)
  Pallas kernels: 87.6 us -> 74.2 us
  local copies, waits for them, and re-layouts: 4.91 us -> 2.87 us
    pallas_call x1, Pallas kernels: 87.6 us -> 74.2 us  [per_device(): pl.pallas_call(kernel, name='polarizability', out_shape=jax.ShapeDtypeStr...]
    unnamed x5 -> x0, local copies, waits for them, and re-layouts: 3.27 us -> none
    transpose x1, local copies, waits for them, and re-layouts: 1.65 us -> 2.87 us  [per_device(): return jnp.transpose(result, (1, 0, 2))]
where the time goes in v3:
time: 77.2 us; the launch traced here: 77 us
  Pallas kernels  74.2 us (96%)
  local copies, waits for them, and re-layouts  2.87 us (4%)
    pallas_call x1, Pallas kernels, per_device(): pl.pallas_call(kernel, name='polarizability', out_shape=jax.ShapeDtypeStr...  74.2 us
    transpose x1, local copies, waits for them, and re-layouts, per_device(): return jnp.transpose(result, (1, 0, 2))  2.87 us

profile of v3, /device:TPU:1, one launch (start us, length us, event | category | flops | bytes accessed | tf_op | source)
XLA Modules:
  0.0 77.0 jit_solution(12873340843759584056)
XLA Ops:
  0.0 74.2 %polarizability.1 = f32[4,128,512]{2,1,0:T(8,128)} custom-call(bf16[6,256,512]{2,1,0:T(8,128)(2,1)} %bitcast.5, bf16[256,1024]{1,0:T(8,128)(2,1)} %bitcast.6, s32[4,4,6]{2,1,0:T(4,128)} %bitcast.7, s32[4]{0:T(128)} %slot_ref.1, f32[4]{0:T(128)} %time_ref.1, f32[4]{0:T(128)} %freq_ref.1, f32[4,4]{1,0:T(4,128)} %cw_ref.1), custom_call_target="tpu_custom_call" | custom-call | flops 9699999744 | bytes 3000000 | tf_op jit(solution)/shard_map/polarizability/pallas_call | solution.py:372
  74.2 2.9 %copy.8 = f32[128,4,512]{2,1,0:T(4,128)} copy(f32[128,4,512]{2,0,1:T(8,128)} %bitcast.4) | data formatting | bytes 2097152 | tf_op jit(solution)/shard_map/transpose | solution.py:415

commit v4 on v3

--- a/solution.py
+++ b/solution.py
@@ -56,7 +56,7 @@
     greet += [dev((x + d) & 3, yh * 2 + 1 - yl, z, c) for d in range(1, 4)]
     greet += [((z + d) & 7, orb, aux) for d in (2, 3, 5, 6)]
     greet += [(z, (y + 4 - (slab >> 2)) & 3, slab) for slab in range(8)]
-    for where in greet:
+    for where in greet[::-1]:
         pl.semaphore_signal(barrier, inc=1, device_id=where, device_id_type=MESH)
 
     load_m.wait()
@@ -272,33 +272,33 @@
                 else:
                     out_ref[j, :, cols] += term
 
-    pass_on()
     load_g.wait()
     g_copy(0).wait_recv()
     es[...] = (0.5 * lax.dot_general(
         gc[...], g_in[...], (((1,), (1,)), ((), ())), preferred_element_type=F32
     )).reshape(2, 64, 256)
     e_copy().start()
+    pass_on()
 
     e_copy().wait_recv()
     smy[...] = (es[keep] + er[...]).astype(BF16)
     for d in range(1, 8):
         plane_copy(d).start()
     sbuf[z, c, aux] = smy[...]
+    for d in range(1, 8):
+        plane_copy(d).wait_recv()
+    z_event(0)
+    first(0)
+    first(1)
+    first(2)
+    second(0)
+    z_event(1)
+    second(1)
+    second(2)
     table = [
         [cw_ref[j, s] * jnp.cos(jnp.full((8, 256), freq_ref[j] * time_ref[s], F32)) for s in range(4)]
         for j in range(4)
     ]
-    first(0)
-    first(1)
-    first(2)
-    for d in range(1, 8):
-        plane_copy(d).wait_recv()
-    z_event(0)
-    second(0)
-    z_event(1)
-    second(1)
-    second(2)
     for n in range(PARTS):
         sib_copy(n).wait_recv()
     z_event(2)

time: 77.2 us -> 73.6 us (0.953)
  Pallas kernels: 74.2 us -> 70.6 us
    pallas_call x1, Pallas kernels: 74.2 us -> 70.6 us  [per_device(): pl.pallas_call(kernel, name='polarizability', out_shape=jax.ShapeDtypeStr...]
where the time goes in v4:
time: 73.6 us; the launch traced here: 73.4 us
  Pallas kernels  70.6 us (96%)
  local copies, waits for them, and re-layouts  2.87 us (4%)
    pallas_call x1, Pallas kernels, per_device(): pl.pallas_call(kernel, name='polarizability', out_shape=jax.ShapeDtypeStr...  70.6 us
    transpose x1, local copies, waits for them, and re-layouts, per_device(): return jnp.transpose(result, (1, 0, 2))  2.87 us

profile of v4, /device:TPU:1, one launch (start us, length us, event | category | flops | bytes accessed | tf_op | source)
XLA Modules:
  0.0 73.4 jit_solution(11168319969682613795)
XLA Ops:
  0.0 70.6 %polarizability.1 = f32[4,128,512]{2,1,0:T(8,128)} custom-call(bf16[6,256,512]{2,1,0:T(8,128)(2,1)} %bitcast.5, bf16[256,1024]{1,0:T(8,128)(2,1)} %bitcast.6, s32[4,4,6]{2,1,0:T(4,128)} %bitcast.7, s32[4]{0:T(128)} %slot_ref.1, f32[4]{0:T(128)} %time_ref.1, f32[4]{0:T(128)} %freq_ref.1, f32[4,4]{1,0:T(4,128)} %cw_ref.1), custom_call_target="tpu_custom_call" | custom-call | flops 9699999744 | bytes 3000000 | tf_op jit(solution)/shard_map/polarizability/pallas_call | solution.py:372
  70.6 2.9 %copy.8 = f32[128,4,512]{2,1,0:T(4,128)} copy(f32[128,4,512]{2,0,1:T(8,128)} %bitcast.4) | data formatting | bytes 2097152 | tf_op jit(solution)/shard_map/transpose | solution.py:415

commit v5 on v4

--- a/solution.py
+++ b/solution.py
@@ -294,6 +294,7 @@
     second(0)
     z_event(1)
     second(1)
+    z_event(2)
     second(2)
     table = [
         [cw_ref[j, s] * jnp.cos(jnp.full((8, 256), freq_ref[j] * time_ref[s], F32)) for s in range(4)]
@@ -301,7 +302,6 @@
     ]
     for n in range(PARTS):
         sib_copy(n).wait_recv()
-    z_event(2)
     sibling_ready(0)
     sibling_ready(1)
     second_done(0)

time: 73.6 us -> 73.6 us (level)
  no operation moved by 1% of the time
where the time goes in v5:
time: 73.6 us; the launch traced here: 73.4 us
  Pallas kernels  70.6 us (96%)
  local copies, waits for them, and re-layouts  2.87 us (4%)
    pallas_call x1, Pallas kernels, per_device(): pl.pallas_call(kernel, name='polarizability', out_shape=jax.ShapeDtypeStr...  70.6 us
    transpose x1, local copies, waits for them, and re-layouts, per_device(): return jnp.transpose(result, (1, 0, 2))  2.87 us

profile of v5, /device:TPU:1, one launch (start us, length us, event | category | flops | bytes accessed | tf_op | source)
XLA Modules:
  0.0 73.4 jit_solution(6198240908390355482)
XLA Ops:
  0.0 70.6 %polarizability.1 = f32[4,128,512]{2,1,0:T(8,128)} custom-call(bf16[6,256,512]{2,1,0:T(8,128)(2,1)} %bitcast.5, bf16[256,1024]{1,0:T(8,128)(2,1)} %bitcast.6, s32[4,4,6]{2,1,0:T(4,128)} %bitcast.7, s32[4]{0:T(128)} %slot_ref.1, f32[4]{0:T(128)} %time_ref.1, f32[4]{0:T(128)} %freq_ref.1, f32[4,4]{1,0:T(4,128)} %cw_ref.1), custom_call_target="tpu_custom_call" | custom-call | flops 9699999744 | bytes 3000000 | tf_op jit(solution)/shard_map/polarizability/pallas_call | solution.py:372
  70.6 2.9 %copy.8 = f32[128,4,512]{2,1,0:T(4,128)} copy(f32[128,4,512]{2,0,1:T(8,128)} %bitcast.4) | data formatting | bytes 2097152 | tf_op jit(solution)/shard_map/transpose | solution.py:415
